TPU v7x, 256 devices: a whole 4x4x8 slice. The times are simulated.
256 devices in a mesh: outer: 32 (over y, x, core), inner: 8 (over z).
Axes of the slice: x: 4, y: 4, z: 8, core: 2. Of those that a mesh axis runs over, the one named last changes fastest.
Arguments:
- query_matrix: bfloat16 [32768, 8192], P(('outer', 'inner')), may hold values from -400 to 400
- key_matrix: bfloat16 [32768, 1024], P(('outer', 'inner')), may hold values from -6 to 6
- value_matrix: bfloat16 [32768, 1024], P(('outer', 'inner')), may hold values from -6 to 6
- output_gradient: bfloat16 [32768, 8192], P(('outer', 'inner')), may hold values from -6 to 6
- doc_ids: int32 [32768], replicated, may hold values from 0 to 127, never falling along the last dimension, each value on 1 to 512 neighbouring positions
Outputs:
- attended: bfloat16 [32768, 8192], P(('outer', 'inner'))
- query_grad: bfloat16 [32768, 8192], P(('outer', 'inner'))
- key_grad: bfloat16 [32768, 1024], P(('outer', 'inner'))
- value_grad: bfloat16 [32768, 1024], P(('outer', 'inner'))
Inputs may be any that keep to these rules, and one draw needn't show every extreme that they name: `doc_ids`: each token's document number; it never falls along the sequence, and a document holds 1 to 512 tokens.
All inputs are finite; a program needn't handle non-finite values.
Results may differ from a plain program's by a relative error of at most 0.039.
Values may be sent and summed in bfloat16 or wider, within the bound.
A program may use at most 128 MiB of HBM per device.

v0:
```python
import jax
import jax.numpy as jnp
from jax import lax
from jax.sharding import PartitionSpec as P

QUERY_HEADS = 64
KEY_VALUE_HEADS = 8
HEAD_SIZE = 128


NEG = -1e30


def passed_along(value, axis, steps):
    count = lax.axis_size(axis)
    pairs = [(source, (source + steps) % count) for source in range(count)]
    return lax.ppermute(value, axis, pairs)


def passed_along_2(value, axis, steps):
    count = lax.axis_size(axis)
    leading, last = (max(0, -steps), min(count, count - steps))
    return lax.ppermute(value, axis, [(source, source + steps) for source in range(leading, last)])


def as_sent(array):
    return jax.tree.map(lambda a: a.astype(jnp.bfloat16) if a.dtype == jnp.float32 else a, array)


def block_info(doc_ids, block_id, row_count):
    block_total = doc_ids.shape[0] // row_count
    safe_block = jnp.clip(block_id, 0, block_total - 1)
    places = block_id * row_count + jnp.arange(row_count, dtype=jnp.int32)
    labels = lax.dynamic_slice_in_dim(doc_ids, safe_block * row_count, row_count)
    usable = jnp.broadcast_to((block_id >= 0) & (block_id < block_total), (row_count,))
    return (places, labels, usable)


def joined(sides):
    return tuple((jnp.concatenate(members) for members in zip(*sides)))


def allowed_pairs(query_side, key_side, row_count):
    query_places, query_labels, query_usable = query_side
    key_places, key_labels, key_usable = key_side
    same_doc = query_labels[:, None] == key_labels[None, :]
    causal = key_places[None, :] <= query_places[:, None]
    within = key_places[None, :] // row_count >= query_places[:, None] // row_count - 2
    return same_doc & causal & within & query_usable[:, None] & key_usable[None, :]


def split_heads(query_template):
    return query_template.reshape(
        query_template.shape[0], KEY_VALUE_HEADS, QUERY_HEADS // KEY_VALUE_HEADS, HEAD_SIZE
    ).transpose(1, 0, 2, 3)


def split_pairs(key_template):
    return key_template.reshape(key_template.shape[0], KEY_VALUE_HEADS, HEAD_SIZE).transpose(
        1, 0, 2
    )


def merge_heads(per_head):
    return per_head.transpose(1, 0, 2, 3).reshape(per_head.shape[1], QUERY_HEADS * HEAD_SIZE)


def head_stats(stats):
    return stats.reshape(QUERY_HEADS, stats.shape[-1]).T


def stats_heads(softmax_statistics):
    return softmax_statistics.T.reshape(
        KEY_VALUE_HEADS, QUERY_HEADS // KEY_VALUE_HEADS, softmax_statistics.shape[0]
    )


def attend_forward(query_matrix, key_matrix, value_matrix, allowed):
    scaling = HEAD_SIZE ** (-0.5)

    def per_group(operands):
        query_group, key_group, value_group = operands
        scores = (
            jnp.einsum("rgd,cd->grc", query_group, key_group, preferred_element_type=jnp.float32)
            * scaling
        )
        scores = jnp.where(allowed[None], scores, NEG)
        highest = jnp.max(scores, axis=-1)
        weights = jnp.where(allowed[None], jnp.exp(scores - highest[..., None]), 0.0)
        totals = jnp.sum(weights, axis=-1)
        partial_out = jnp.einsum(
            "grc,cd->rgd",
            weights.astype(jnp.bfloat16),
            value_group,
            preferred_element_type=jnp.float32,
        )
        return (partial_out, highest, totals)

    partial_out, highest, totals = lax.map(
        per_group, (split_heads(query_matrix), split_pairs(key_matrix), split_pairs(value_matrix))
    )
    return (merge_heads(partial_out), head_stats(highest), head_stats(totals))


def attend_backward(query_matrix, key_matrix, value_matrix, grad_rows, log_total, row_dot, allowed):
    scaling = HEAD_SIZE ** (-0.5)
    key_total_count = key_matrix.shape[0]

    def per_group(operands):
        query_group, key_group, value_group, grad_group, log_group, dot_group = operands
        scores = (
            jnp.einsum("rgd,cd->grc", query_group, key_group, preferred_element_type=jnp.float32)
            * scaling
        )
        probs = jnp.where(allowed[None], jnp.exp(scores - log_group[..., None]), 0.0)
        grad_weights = jnp.einsum(
            "rgd,cd->grc", grad_group, value_group, preferred_element_type=jnp.float32
        )
        grad_coarse = (probs * (grad_weights - dot_group[..., None])).astype(jnp.bfloat16)
        value_portion = jnp.einsum(
            "grc,rgd->cd",
            probs.astype(jnp.bfloat16),
            grad_group,
            preferred_element_type=jnp.float32,
        )
        key_portion = (
            jnp.einsum("grc,rgd->cd", grad_coarse, query_group, preferred_element_type=jnp.float32)
            * scaling
        )
        query_part = (
            jnp.einsum("grc,cd->rgd", grad_coarse, key_group, preferred_element_type=jnp.float32)
            * scaling
        )
        return (query_part, key_portion, value_portion)

    query_part, key_portion, value_portion = lax.map(
        per_group,
        (
            split_heads(query_matrix),
            split_pairs(key_matrix),
            split_pairs(value_matrix),
            split_heads(grad_rows),
            stats_heads(log_total),
            stats_heads(row_dot),
        ),
    )
    return (
        merge_heads(query_part),
        key_portion.transpose(1, 0, 2).reshape(key_total_count, KEY_VALUE_HEADS * HEAD_SIZE),
        value_portion.transpose(1, 0, 2).reshape(key_total_count, KEY_VALUE_HEADS * HEAD_SIZE),
    )


def finish(numerator, highest, totals, output_gradient):
    row_count = numerator.shape[0]
    attended = (
        (numerator / totals[..., None])
        .reshape(row_count, QUERY_HEADS * HEAD_SIZE)
        .astype(jnp.bfloat16)
    )
    log_total = highest + jnp.log(totals)
    row_dot = jnp.sum(
        output_gradient.astype(jnp.float32).reshape(row_count, QUERY_HEADS, HEAD_SIZE)
        * attended.astype(jnp.float32).reshape(row_count, QUERY_HEADS, HEAD_SIZE),
        axis=-1,
    )
    return (attended, log_total, row_dot)


def body(query_matrix, key_matrix, value_matrix, output_gradient, doc_ids):
    row_count = query_matrix.shape[0]
    inner_count = lax.axis_size("inner")
    outer_place = lax.axis_index("outer")
    inner_place = lax.axis_index("inner")
    own_block = outer_place * inner_count + inner_place
    near_block = outer_place * inner_count + (inner_place + inner_count - 1) % inner_count
    far_block = outer_place * inner_count + (inner_place + inner_count - 2) % inner_count
    moving = (key_matrix, value_matrix)
    fetched = []
    for cycle_step in range(2):
        moving = passed_along((moving[0], moving[1]), "inner", 1)
        fetched.append(moving)
    near_pair, far_pair = fetched
    own_side = block_info(doc_ids, own_block, row_count)
    near_side = block_info(doc_ids, near_block, row_count)
    far_side = block_info(doc_ids, far_block, row_count)
    guest_blocks = passed_along_2(
        (near_pair[0], near_pair[1], far_pair[0], far_pair[1]), "outer", 1
    )
    key_side = joined(
        [
            own_side,
            near_side,
            far_side,
            block_info(doc_ids, near_block - inner_count, row_count),
            block_info(doc_ids, far_block - inner_count, row_count),
        ]
    )
    allowed = allowed_pairs(own_side, key_side, row_count)
    all_keys = jnp.concatenate(
        [key_matrix, near_pair[0], far_pair[0], guest_blocks[0], guest_blocks[2]]
    )
    all_values = jnp.concatenate(
        [value_matrix, near_pair[1], far_pair[1], guest_blocks[1], guest_blocks[3]]
    )
    part_rows, highest, totals = attend_forward(query_matrix, all_keys, all_values, allowed)
    attended, log_total, row_dot = finish(
        part_rows.reshape(row_count, QUERY_HEADS, HEAD_SIZE), highest, totals, output_gradient
    )
    query_grad, key_portion, value_portion = attend_backward(
        query_matrix, all_keys, all_values, output_gradient, log_total, row_dot, allowed
    )
    returned = (
        passed_along_2(
            key_portion[3 * row_count : 4 * row_count].astype(jnp.bfloat16), "outer", -1
        ).astype(jnp.float32),
        passed_along_2(
            value_portion[3 * row_count : 4 * row_count].astype(jnp.bfloat16), "outer", -1
        ).astype(jnp.float32),
        passed_along_2(key_portion[4 * row_count :].astype(jnp.bfloat16), "outer", -1).astype(
            jnp.float32
        ),
        passed_along_2(value_portion[4 * row_count :].astype(jnp.bfloat16), "outer", -1).astype(
            jnp.float32
        ),
    )
    key_portion = jnp.concatenate(
        [
            key_portion[:row_count],
            key_portion[row_count : 2 * row_count] + returned[0],
            key_portion[2 * row_count : 3 * row_count] + returned[2],
        ]
    )
    value_portion = jnp.concatenate(
        [
            value_portion[:row_count],
            value_portion[row_count : 2 * row_count] + returned[1],
            value_portion[2 * row_count : 3 * row_count] + returned[3],
        ]
    )
    own_key = key_portion[:row_count]
    own_value = value_portion[:row_count]
    near_key = key_portion[row_count : 2 * row_count]
    near_value = value_portion[row_count : 2 * row_count]
    far_key = key_portion[2 * row_count : 3 * row_count]
    far_value = value_portion[2 * row_count : 3 * row_count]
    moving = (far_key, far_value)
    for cycle_step in range(2):
        moving = passed_along((as_sent(moving[0]), as_sent(moving[1])), "inner", -1)
        if cycle_step == 0:
            moving = (moving[0] + near_key, moving[1] + near_value)
    key_grad = own_key + moving[0]
    value_grad = own_value + moving[1]
    return (
        attended,
        query_grad.astype(jnp.bfloat16),
        key_grad.astype(jnp.bfloat16),
        value_grad.astype(jnp.bfloat16),
    )


def solution(mesh):
    return jax.shard_map(
        body,
        mesh=mesh,
        in_specs=(
            P(("outer", "inner"), None),
            P(("outer", "inner"), None),
            P(("outer", "inner"), None),
            P(("outer", "inner"), None),
            P(),
        ),
        out_specs=(
            P(("outer", "inner"), None),
            P(("outer", "inner"), None),
            P(("outer", "inner"), None),
            P(("outer", "inner"), None),
        ),
        check_vma=False,
    )
```

profile of v0, /device:TPU:24, one launch (start us, length us, event | category | flops | bytes accessed | tf_op | source)
XLA Modules:
  0.0 224.8 jit_solution(8077484484033904931)
XLA Ops:
  6.1 1.9 collective-permute-start
  12.9 4.0 %convert_bitcast_fusion = f32[16,8,64,128]{3,1,2,0:T(8,128)} fusion(bf16[128,8192]{1,0:T(8,128)(2,1)} %param.12), kind=kLoop, calls=%fused_computation.71 | loop fusion | flops 1048576 | bytes 6291456
  20.6 1.9 collective-permute-start.5
  22.6 2.4 %copy.98 = bf16[128,8192]{0,1:T(8,128)(2,1)} copy(bf16[128,8192]{1,0:T(8,128)(2,1)S(1)} %copy-done.1) | data formatting | bytes 4194304 | tf_op args[3]
  25.1 4.1 %copy.93 = bf16[128,8192]{0,1:T(8,128)(2,1)} copy(bf16[128,8192]{1,0:T(8,128)(2,1)} %param.9) | data formatting | bytes 4194304 | tf_op args[0]
  29.1 3.0 %copy.95 = bf16[8,128,8,128]{3,1,2,0:T(8,128)(2,1)S(1)} copy(bf16[8,128,8,128]{1,3,2,0:T(8,128)(2,1)} %bitcast.290) | data formatting | bytes 4194304
  32.2 4.9 %copy.135 = f32[16,8,64,128]{3,2,1,0:T(8,128)} copy(f32[16,8,64,128]{3,1,2,0:T(8,128)} %convert_bitcast_fusion) | data formatting | bytes 8388608
  40.1 3.2 %collective-permute-start.1 = (bf16[128,1024]{0,1:T(8,128)(2,1)}, bf16[128,1024]{0,1:T(8,128)(2,1)}, u32[]{:S(2)}, u32[]{:S(2)}) collective-permute-start(bf16[128,1024]{0,1:T(8,128)(2,1)} %collective-permute-done), channel_id=1, source_target_pairs={{0,1},{1,2},{2,3},{3,4},{4,5},{5,6},{6,7},{7,0},{8,9},{9,10},{10,1... | collective-permute-start | bytes 786440 | tf_op jit(solution)/shard_map/ppermute | solution.py:17
  43.3 3.2 %collective-permute-start.2 = (bf16[128,1024]{0,1:T(8,128)(2,1)}, bf16[128,1024]{0,1:T(8,128)(2,1)S(1)}, u32[]{:S(2)}, u32[]{:S(2)}) collective-permute-start(bf16[128,1024]{0,1:T(8,128)(2,1)} %collective-permute-done), channel_id=1, source_target_pairs={{0,8},{8,16},{16,24},{24,32},{32,40},{40,48},{48,56},{56,64},{64,7... | collective-permute-start | bytes 786440 | tf_op jit(solution)/shard_map/ppermute | solution.py:23
  49.2 2.2 collective-permute-start.7
  52.4 3.4 %collective-permute-start.3 = (bf16[128,1024]{0,1:T(8,128)(2,1)}, bf16[128,1024]{0,1:T(8,128)(2,1)}, u32[]{:S(2)}, u32[]{:S(2)}) collective-permute-start(bf16[128,1024]{0,1:T(8,128)(2,1)} %collective-permute-done.1), channel_id=1, source_target_pairs={{0,8},{8,16},{16,24},{24,32},{32,40},{40,48},{48,56},{56,64},{64,7... | collective-permute-start | bytes 786440 | tf_op jit(solution)/shard_map/ppermute | solution.py:23
  64.2 40.0 %while.32 = (s32[]{:T(128)}, f32[8,128,8,128]{1,3,2,0:T(8,128)}, f32[8,8,128]{2,1,0:T(8,128)}, f32[8,8,128]{2,1,0:T(8,128)S(1)}, bf16[8,640,128]{1,2,0:T(8,128)(...) while((s32[]{:T(128)}, f32[8,128,8,128]{1,3,2,0:T(8,128)}, ...), condition=%wide.region_3.4_spmd.clone.clone, body=%wide.region_0.3_spmd.clone.sunk.clone | while | flops 344635392 | bytes 9351438 | solution.py:99
  66.7 2.5 %fusion.126 = f32[8,128,8,128]{1,3,2,0:T(8,128)} fusion(f32[8,128,8,128]{1,3,2,0:T(8,128)} %get-tuple-element.705, s32[]{:T(128)} %get-tuple-element.704, f32[640,128,8]{1,0,2:T(8,128)S(1)} %get-tuple-element.629, f32[8,128]{1,0:T(8,128)S(1)} %get-tuple-element.630, pred[128,640]{0,1:T(8,128)(4,1)S(1)} %and_and_fusion.6, ...), kind=kOutput, calls=%fused_computation.10.clone.1.clone | convolution fusion | flops 171048960 | bytes 3396608 | tf_op jit(solution)/shard_map/while/body/eval_jaxpr/grc,cd->rgd/dot_general | solution.py:91
  71.7 2.5 %fusion.126 = f32[8,128,8,128]{1,3,2,0:T(8,128)} fusion(f32[8,128,8,128]{1,3,2,0:T(8,128)} %get-tuple-element.705, s32[]{:T(128)} %get-tuple-element.704, f32[640,128,8]{1,0,2:T(8,128)S(1)} %get-tuple-element.629, f32[8,128]{1,0:T(8,128)S(1)} %get-tuple-element.630, pred[128,640]{0,1:T(8,128)(4,1)S(1)} %and_and_fusion.6, ...), kind=kOutput, calls=%fused_computation.10.clone.1.clone | convolution fusion | flops 171048960 | bytes 3396608 | tf_op jit(solution)/shard_map/while/body/eval_jaxpr/grc,cd->rgd/dot_general | solution.py:91
  76.7 2.5 %fusion.126 = f32[8,128,8,128]{1,3,2,0:T(8,128)} fusion(f32[8,128,8,128]{1,3,2,0:T(8,128)} %get-tuple-element.705, s32[]{:T(128)} %get-tuple-element.704, f32[640,128,8]{1,0,2:T(8,128)S(1)} %get-tuple-element.629, f32[8,128]{1,0:T(8,128)S(1)} %get-tuple-element.630, pred[128,640]{0,1:T(8,128)(4,1)S(1)} %and_and_fusion.6, ...), kind=kOutput, calls=%fused_computation.10.clone.1.clone | convolution fusion | flops 171048960 | bytes 3396608 | tf_op jit(solution)/shard_map/while/body/eval_jaxpr/grc,cd->rgd/dot_general | solution.py:91
  81.7 2.5 %fusion.126 = f32[8,128,8,128]{1,3,2,0:T(8,128)} fusion(f32[8,128,8,128]{1,3,2,0:T(8,128)} %get-tuple-element.705, s32[]{:T(128)} %get-tuple-element.704, f32[640,128,8]{1,0,2:T(8,128)S(1)} %get-tuple-element.629, f32[8,128]{1,0:T(8,128)S(1)} %get-tuple-element.630, pred[128,640]{0,1:T(8,128)(4,1)S(1)} %and_and_fusion.6, ...), kind=kOutput, calls=%fused_computation.10.clone.1.clone | convolution fusion | flops 171048960 | bytes 3396608 | tf_op jit(solution)/shard_map/while/body/eval_jaxpr/grc,cd->rgd/dot_general | solution.py:91
  86.7 2.5 %fusion.126 = f32[8,128,8,128]{1,3,2,0:T(8,128)} fusion(f32[8,128,8,128]{1,3,2,0:T(8,128)} %get-tuple-element.705, s32[]{:T(128)} %get-tuple-element.704, f32[640,128,8]{1,0,2:T(8,128)S(1)} %get-tuple-element.629, f32[8,128]{1,0:T(8,128)S(1)} %get-tuple-element.630, pred[128,640]{0,1:T(8,128)(4,1)S(1)} %and_and_fusion.6, ...), kind=kOutput, calls=%fused_computation.10.clone.1.clone | convolution fusion | flops 171048960 | bytes 3396608 | tf_op jit(solution)/shard_map/while/body/eval_jaxpr/grc,cd->rgd/dot_general | solution.py:91
  91.7 2.5 %fusion.126 = f32[8,128,8,128]{1,3,2,0:T(8,128)} fusion(f32[8,128,8,128]{1,3,2,0:T(8,128)} %get-tuple-element.705, s32[]{:T(128)} %get-tuple-element.704, f32[640,128,8]{1,0,2:T(8,128)S(1)} %get-tuple-element.629, f32[8,128]{1,0:T(8,128)S(1)} %get-tuple-element.630, pred[128,640]{0,1:T(8,128)(4,1)S(1)} %and_and_fusion.6, ...), kind=kOutput, calls=%fused_computation.10.clone.1.clone | convolution fusion | flops 171048960 | bytes 3396608 | tf_op jit(solution)/shard_map/while/body/eval_jaxpr/grc,cd->rgd/dot_general | solution.py:91
  96.7 2.5 %fusion.126 = f32[8,128,8,128]{1,3,2,0:T(8,128)} fusion(f32[8,128,8,128]{1,3,2,0:T(8,128)} %get-tuple-element.705, s32[]{:T(128)} %get-tuple-element.704, f32[640,128,8]{1,0,2:T(8,128)S(1)} %get-tuple-element.629, f32[8,128]{1,0:T(8,128)S(1)} %get-tuple-element.630, pred[128,640]{0,1:T(8,128)(4,1)S(1)} %and_and_fusion.6, ...), kind=kOutput, calls=%fused_computation.10.clone.1.clone | convolution fusion | flops 171048960 | bytes 3396608 | tf_op jit(solution)/shard_map/while/body/eval_jaxpr/grc,cd->rgd/dot_general | solution.py:91
  101.7 2.6 %fusion.126 = f32[8,128,8,128]{1,3,2,0:T(8,128)} fusion(f32[8,128,8,128]{1,3,2,0:T(8,128)} %get-tuple-element.705, s32[]{:T(128)} %get-tuple-element.704, f32[640,128,8]{1,0,2:T(8,128)S(1)} %get-tuple-element.629, f32[8,128]{1,0:T(8,128)S(1)} %get-tuple-element.630, pred[128,640]{0,1:T(8,128)(4,1)S(1)} %and_and_fusion.6, ...), kind=kOutput, calls=%fused_computation.10.clone.1.clone | convolution fusion | flops 171048960 | bytes 3396608 | tf_op jit(solution)/shard_map/while/body/eval_jaxpr/grc,cd->rgd/dot_general | solution.py:91
  104.3 5.4 %copy.99 = f32[128,64,128]{2,1,0:T(8,128)} copy(f32[128,64,128]{0,2,1:T(8,128)} %bitcast.15) | data formatting | bytes 8388608 | tf_op jit(solution)/shard_map/reshape;reshape | solution.py:208
  109.8 4.7 %multiply_reduce_fusion = f32[128,64]{1,0:T(8,128)S(1)} fusion(f32[128,64,128]{2,1,0:T(8,128)} %bitcast.287, f32[128,64,128]{2,1,0:T(8,128)} %copy.99, f32[128,64]{1,0:T(8,128)S(1)} %copy.97), kind=kLoop, calls=%fused_computation.72 | loop fusion | flops 5234688 | bytes 8454144 | tf_op jit(solution)/shard_map/reduce_sum | solution.py:162
  116.0 68.1 %while.33 = (s32[]{:T(128)}, bf16[8,128,8,128]{1,3,2,0:T(8,128)(2,1)}, f32[8,640,128]{2,1,0:T(8,128)}, f32[8,640,128]{2,1,0:T(8,128)}, bf16[8,640,128]{2,1,0:T(8...) while((s32[]{:T(128)}, ...), condition=%wide.region_6.7_spmd.clone.clone, body=%wide.region_5.6_spmd.clone.sunk.clone | while | flops 846200832 | bytes 14812030 | solution.py:136
  117.9 2.0 fusion.139
  122.3 2.3 %fusion.142 = f32[8,640,128]{2,1,0:T(8,128)} fusion(f32[8,640,128]{2,1,0:T(8,128)} %get-tuple-element.755, s32[]{:T(128)} %get-tuple-element.752, f32[640,128,8]{1,0,2:T(8,128)S(1)} %fusion.138, f32[8,128]{1,0:T(8,128)S(1)} %get-tuple-element.669, pred[128,640]{0,1:T(8,128)(4,1)S(1)} %and_and_fusion.7, ...), kind=kOutput, calls=%fused_computation.39.clone.1.clone | convolution fusion | flops 170393600 | bytes 3298304 | tf_op jit(solution)/shard_map/while/body/eval_jaxpr/grc,rgd->cd/dot_general | solution.py:120
  126.5 1.9 fusion.139
  130.8 2.2 fusion.142
  135.0 1.9 fusion.139
  139.3 2.3 %fusion.142 = f32[8,640,128]{2,1,0:T(8,128)} fusion(f32[8,640,128]{2,1,0:T(8,128)} %get-tuple-element.755, s32[]{:T(128)} %get-tuple-element.752, f32[640,128,8]{1,0,2:T(8,128)S(1)} %fusion.138, f32[8,128]{1,0:T(8,128)S(1)} %get-tuple-element.669, pred[128,640]{0,1:T(8,128)(4,1)S(1)} %and_and_fusion.7, ...), kind=kOutput, calls=%fused_computation.39.clone.1.clone | convolution fusion | flops 170393600 | bytes 3298304 | tf_op jit(solution)/shard_map/while/body/eval_jaxpr/grc,rgd->cd/dot_general | solution.py:120
  143.5 1.9 fusion.139
  147.8 2.2 fusion.142
  152.0 1.9 fusion.139
  156.3 2.2 fusion.142
  160.4 2.0 fusion.139
  164.8 2.3 %fusion.142 = f32[8,640,128]{2,1,0:T(8,128)} fusion(f32[8,640,128]{2,1,0:T(8,128)} %get-tuple-element.755, s32[]{:T(128)} %get-tuple-element.752, f32[640,128,8]{1,0,2:T(8,128)S(1)} %fusion.138, f32[8,128]{1,0:T(8,128)S(1)} %get-tuple-element.669, pred[128,640]{0,1:T(8,128)(4,1)S(1)} %and_and_fusion.7, ...), kind=kOutput, calls=%fused_computation.39.clone.1.clone | convolution fusion | flops 170393600 | bytes 3298304 | tf_op jit(solution)/shard_map/while/body/eval_jaxpr/grc,rgd->cd/dot_general | solution.py:120
  169.0 1.9 fusion.139
  173.3 2.2 fusion.142
  177.5 1.9 fusion.139
  181.8 2.3 %fusion.142 = f32[8,640,128]{2,1,0:T(8,128)} fusion(f32[8,640,128]{2,1,0:T(8,128)} %get-tuple-element.755, s32[]{:T(128)} %get-tuple-element.752, f32[640,128,8]{1,0,2:T(8,128)S(1)} %fusion.138, f32[8,128]{1,0:T(8,128)S(1)} %get-tuple-element.669, pred[128,640]{0,1:T(8,128)(4,1)S(1)} %and_and_fusion.7, ...), kind=kOutput, calls=%fused_computation.39.clone.1.clone | convolution fusion | flops 170393600 | bytes 3298304 | tf_op jit(solution)/shard_map/while/body/eval_jaxpr/grc,rgd->cd/dot_general | solution.py:120
  184.0 2.1 bitcast_convert_fusion
  186.3 3.2 %collective-permute-start.12 = (bf16[128,1024]{1,0:T(8,128)(2,1)S(1)}, bf16[128,1024]{1,0:T(8,128)(2,1)S(1)}, u32[]{:S(2)}, u32[]{:S(2)}) collective-permute-start(bf16[128,1024]{1,0:T(8,128)(2,1)S(1)} %bitcast.296), channel_id=1, source_target_pairs={{8,0},{16,8},{24,16},{32,24},{40,32},{48,40},{56,48},{64,56},{72,6... | collective-permute-start | bytes 786440 | tf_op jit(solution)/shard_map/ppermute | solution.py:23
  190.2 2.1 collective-permute-start.14
  192.7 2.3 %collective-permute-start.8 = (bf16[128,1024]{1,0:T(8,128)(2,1)S(1)}, bf16[128,1024]{1,0:T(8,128)(2,1)S(1)}, u32[]{:S(2)}, u32[]{:S(2)}) collective-permute-start(bf16[128,1024]{1,0:T(8,128)(2,1)S(1)} %bitcast.295), channel_id=1, source_target_pairs={{8,0},{16,8},{24,16},{32,24},{40,32},{48,40},{56,48},{64,56},{72,6... | collective-permute-start | bytes 786440 | tf_op jit(solution)/shard_map/ppermute | solution.py:23
  198.3 2.6 %collective-permute-start.10 = (bf16[128,1024]{1,0:T(8,128)(2,1)}, bf16[128,1024]{1,0:T(8,128)(2,1)S(1)}, u32[]{:S(2)}, u32[]{:S(2)}) collective-permute-start(bf16[128,1024]{1,0:T(8,128)(2,1)} %bitcast.210), channel_id=1, source_target_pairs={{8,0},{16,8},{24,16},{32,24},{40,32},{48,40},{56,48},{64,56},{72,6... | collective-permute-start | bytes 786440 | tf_op jit(solution)/shard_map/ppermute | solution.py:23
  201.8 5.7 %copy.119 = f32[128,8192]{1,0:T(8,128)} copy(f32[128,8192]{0,1:T(8,128)} %bitcast.7) | data formatting | bytes 8388608 | tf_op jit(solution)/shard_map/reshape;reshape | solution.py:208
  209.0 2.9 %collective-permute-done.9 = bf16[128,1024]{1,0:T(8,128)(2,1)S(1)} collective-permute-done((bf16[128,1024]{1,0:T(8,128)(2,1)}, bf16[128,1024]{1,0:T(8,128)(2,1)S(1)}, u32[]{:S(2)}, u32[]{:S(2)}) %collective-permute-start.9) | collective-permute-done | bytes 262176 | tf_op jit(solution)/shard_map/ppermute | solution.py:17
  214.6 3.9 %fusion.69 = bf16[128,8192]{1,0:T(8,128)(2,1)} fusion(f32[128,8192]{1,0:T(8,128)S(1)} %copy-done, f32[16,8,64,128]{3,2,1,0:T(8,128)S(1)} %bitcast.288), kind=kLoop, calls=%fused_computation.70 | loop fusion | flops 2097152 | bytes 10485760 | tf_op jit(solution)/shard_map/convert_element_type | solution.py:159
  218.5 2.9 %copy.120 = bf16[128,8192]{1,0:T(8,128)(2,1)} copy(bf16[128,8192]{0,1:T(8,128)(2,1)S(1)} %bitcast.289) | data formatting | bytes 4194304 | tf_op jit(solution)/shard_map/convert_element_type | solution.py:256
  (221 shorter events, 97.4 us)
Async XLA Ops:
  2.4 18.2 %collective-permute-start.4 = (bf16[128,1024]{0,1:T(8,128)(2,1)}, bf16[128,1024]{0,1:T(8,128)(2,1)}, u32[]{:S(2)}, u32[]{:S(2)}) collective-permute-start(bf16[128,1024]{0,1:T(8,128)(2,1)} %copy.92), channel_id=1, source_target_pairs={{0,1},{1,2},{2,3},{3,4},{4,5},{5,6},{6,7},{7,0},{8,9},{9,10},{10,1... | collective-permute-start | bytes 786440 | tf_op jit(solution)/shard_map/ppermute | solution.py:17
  6.1 33.9 %collective-permute-start = (bf16[128,1024]{0,1:T(8,128)(2,1)}, bf16[128,1024]{0,1:T(8,128)(2,1)}, u32[]{:S(2)}, u32[]{:S(2)}) collective-permute-start(bf16[128,1024]{0,1:T(8,128)(2,1)} %copy.90), channel_id=1, source_target_pairs={{0,1},{1,2},{2,3},{3,4},{4,5},{5,6},{6,7},{7,0},{8,9},{9,10},{10,1... | collective-permute-start | bytes 786440 | tf_op jit(solution)/shard_map/ppermute | solution.py:17
  16.9 5.7 %copy-start.1 = (bf16[128,8192]{1,0:T(8,128)(2,1)S(1)}, bf16[128,8192]{1,0:T(8,128)(2,1)}, u32[]{:S(2)}) copy-start(bf16[128,8192]{1,0:T(8,128)(2,1)} %param.12) | copy-start | bytes 6291460
  20.6 28.6 %collective-permute-start.5 = (bf16[128,1024]{0,1:T(8,128)(2,1)}, bf16[128,1024]{0,1:T(8,128)(2,1)}, u32[]{:S(2)}, u32[]{:S(2)}) collective-permute-start(bf16[128,1024]{0,1:T(8,128)(2,1)} %collective-permute-done.4), channel_id=1, source_target_pairs={{0,1},{1,2},{2,3},{3,4},{4,5},{5,6},{6,7},{7,0},{8,9},{9,10},{10,1... | collective-permute-start | bytes 786440 | tf_op jit(solution)/shard_map/ppermute | solution.py:17
  38.1 19.4 %collective-permute-start.6 = (bf16[128,1024]{0,1:T(8,128)(2,1)}, bf16[128,1024]{0,1:T(8,128)(2,1)S(1)}, u32[]{:S(2)}, u32[]{:S(2)}) collective-permute-start(bf16[128,1024]{0,1:T(8,128)(2,1)} %collective-permute-done.4), channel_id=1, source_target_pairs={{0,8},{8,16},{16,24},{24,32},{32,40},{40,48},{48,56},{56,64},{64,7... | collective-permute-start | bytes 786440 | tf_op jit(solution)/shard_map/ppermute | solution.py:23
  40.1 12.4 %collective-permute-start.1 = (bf16[128,1024]{0,1:T(8,128)(2,1)}, bf16[128,1024]{0,1:T(8,128)(2,1)}, u32[]{:S(2)}, u32[]{:S(2)}) collective-permute-start(bf16[128,1024]{0,1:T(8,128)(2,1)} %collective-permute-done), channel_id=1, source_target_pairs={{0,1},{1,2},{2,3},{3,4},{4,5},{5,6},{6,7},{7,0},{8,9},{9,10},{10,1... | collective-permute-start | bytes 786440 | tf_op jit(solution)/shard_map/ppermute | solution.py:17
  43.3 14.3 %collective-permute-start.2 = (bf16[128,1024]{0,1:T(8,128)(2,1)}, bf16[128,1024]{0,1:T(8,128)(2,1)S(1)}, u32[]{:S(2)}, u32[]{:S(2)}) collective-permute-start(bf16[128,1024]{0,1:T(8,128)(2,1)} %collective-permute-done), channel_id=1, source_target_pairs={{0,8},{8,16},{16,24},{24,32},{32,40},{40,48},{48,56},{56,64},{64,7... | collective-permute-start | bytes 786440 | tf_op jit(solution)/shard_map/ppermute | solution.py:23
  49.2 10.0 %collective-permute-start.7 = (bf16[128,1024]{0,1:T(8,128)(2,1)}, bf16[128,1024]{0,1:T(8,128)(2,1)S(1)}, u32[]{:S(2)}, u32[]{:S(2)}) collective-permute-start(bf16[128,1024]{0,1:T(8,128)(2,1)} %collective-permute-done.5), channel_id=1, source_target_pairs={{0,8},{8,16},{16,24},{24,32},{32,40},{40,48},{48,56},{56,64},{64,7... | collective-permute-start | bytes 786440 | tf_op jit(solution)/shard_map/ppermute | solution.py:23
  52.4 10.1 %collective-permute-start.3 = (bf16[128,1024]{0,1:T(8,128)(2,1)}, bf16[128,1024]{0,1:T(8,128)(2,1)}, u32[]{:S(2)}, u32[]{:S(2)}) collective-permute-start(bf16[128,1024]{0,1:T(8,128)(2,1)} %collective-permute-done.1), channel_id=1, source_target_pairs={{0,8},{8,16},{16,24},{24,32},{32,40},{40,48},{48,56},{56,64},{64,7... | collective-permute-start | bytes 786440 | tf_op jit(solution)/shard_map/ppermute | solution.py:23
  104.3 5.4 %copy-start.6 = (s32[128]{0:T(128)}, s32[128]{0:T(128)S(1)}, u32[]{:S(2)}) copy-start(s32[128]{0:T(128)S(1)} %get-tuple-element.806) | copy-start | bytes 1540
  104.3 5.4 %copy-start.8 = (s32[128]{0:T(128)}, s32[128]{0:T(128)S(1)}, u32[]{:S(2)}) copy-start(s32[128]{0:T(128)S(1)} %get-tuple-element.808) | copy-start | bytes 1540
  104.3 5.4 %copy-start.10 = (s32[128]{0:T(128)}, s32[128]{0:T(128)S(1)}, u32[]{:S(2)}) copy-start(s32[128]{0:T(128)S(1)} %get-tuple-element.809) | copy-start | bytes 1540
  104.3 5.4 %copy-start.5 = (f32[8,8,128]{2,1,0:T(8,128)}, f32[8,8,128]{2,1,0:T(8,128)S(1)}, u32[]{:S(2)}) copy-start(f32[8,8,128]{2,1,0:T(8,128)S(1)} %get-tuple-element.108) | copy-start | bytes 98308
  116.0 1.2 copy-start.7
  116.0 1.2 copy-start.9
  116.0 1.2 copy-start.11
  124.5 1.2 copy-start.7
  124.5 1.2 copy-start.9
  124.5 1.2 copy-start.11
  133.1 1.2 copy-start.7
  133.1 1.2 copy-start.9
  133.1 1.2 copy-start.11
  141.5 1.2 copy-start.7
  141.5 1.2 copy-start.9
  141.5 1.2 copy-start.11
  150.0 1.2 copy-start.7
  150.0 1.2 copy-start.9
  150.0 1.2 copy-start.11
  158.5 1.2 copy-start.7
  158.5 1.2 copy-start.9
  158.5 1.2 copy-start.11
  167.0 1.2 copy-start.7
  167.0 1.2 copy-start.9
  167.0 1.2 copy-start.11
  175.5 1.2 copy-start.7
  175.5 1.2 copy-start.9
  175.5 1.2 copy-start.11
  184.0 8.3 %copy-start.3 = (f32[8,640,128]{2,1,0:T(8,128)S(1)}, f32[8,640,128]{2,1,0:T(8,128)}, u32[]{:S(2)}) copy-start(f32[8,640,128]{2,1,0:T(8,128)} %get-tuple-element.111) | copy-start | bytes 7864324
  186.3 10.2 %collective-permute-start.12 = (bf16[128,1024]{1,0:T(8,128)(2,1)S(1)}, bf16[128,1024]{1,0:T(8,128)(2,1)S(1)}, u32[]{:S(2)}, u32[]{:S(2)}) collective-permute-start(bf16[128,1024]{1,0:T(8,128)(2,1)S(1)} %bitcast.296), channel_id=1, source_target_pairs={{8,0},{16,8},{24,16},{32,24},{40,32},{48,40},{56,48},{64,56},{72,6... | collective-permute-start | bytes 786440 | tf_op jit(solution)/shard_map/ppermute | solution.py:23
  190.2 17.2 %collective-permute-start.14 = (bf16[128,1024]{1,0:T(8,128)(2,1)}, bf16[128,1024]{1,0:T(8,128)(2,1)S(1)}, u32[]{:S(2)}, u32[]{:S(2)}) collective-permute-start(bf16[128,1024]{1,0:T(8,128)(2,1)} %bitcast.208), channel_id=1, source_target_pairs={{8,0},{16,8},{24,16},{32,24},{40,32},{48,40},{56,48},{64,56},{72,6... | collective-permute-start | bytes 786440 | tf_op jit(solution)/shard_map/ppermute | solution.py:23
  192.7 8.2 %collective-permute-start.8 = (bf16[128,1024]{1,0:T(8,128)(2,1)S(1)}, bf16[128,1024]{1,0:T(8,128)(2,1)S(1)}, u32[]{:S(2)}, u32[]{:S(2)}) collective-permute-start(bf16[128,1024]{1,0:T(8,128)(2,1)S(1)} %bitcast.295), channel_id=1, source_target_pairs={{8,0},{16,8},{24,16},{32,24},{40,32},{48,40},{56,48},{64,56},{72,6... | collective-permute-start | bytes 786440 | tf_op jit(solution)/shard_map/ppermute | solution.py:23
  197.3 10.2 %collective-permute-start.13 = (bf16[128,1024]{1,0:T(8,128)(2,1)}, bf16[128,1024]{1,0:T(8,128)(2,1)S(1)}, u32[]{:S(2)}, u32[]{:S(2)}) collective-permute-start(bf16[128,1024]{1,0:T(8,128)(2,1)} %fusion.72), channel_id=1, source_target_pairs={{0,7},{1,0},{2,1},{3,2},{4,3},{5,4},{6,5},{7,6},{8,15},{9,8},{10,9... | collective-permute-start | bytes 786440 | tf_op jit(solution)/shard_map/ppermute | solution.py:17
  198.3 10.7 %collective-permute-start.10 = (bf16[128,1024]{1,0:T(8,128)(2,1)}, bf16[128,1024]{1,0:T(8,128)(2,1)S(1)}, u32[]{:S(2)}, u32[]{:S(2)}) collective-permute-start(bf16[128,1024]{1,0:T(8,128)(2,1)} %bitcast.210), channel_id=1, source_target_pairs={{8,0},{16,8},{24,16},{32,24},{40,32},{48,40},{56,48},{64,56},{72,6... | collective-permute-start | bytes 786440 | tf_op jit(solution)/shard_map/ppermute | solution.py:23
  201.7 10.2 %collective-permute-start.9 = (bf16[128,1024]{1,0:T(8,128)(2,1)}, bf16[128,1024]{1,0:T(8,128)(2,1)S(1)}, u32[]{:S(2)}, u32[]{:S(2)}) collective-permute-start(bf16[128,1024]{1,0:T(8,128)(2,1)} %fusion.76), channel_id=1, source_target_pairs={{0,7},{1,0},{2,1},{3,2},{4,3},{5,4},{6,5},{7,6},{8,15},{9,8},{10,9... | collective-permute-start | bytes 786440 | tf_op jit(solution)/shard_map/ppermute | solution.py:17
  208.3 13.1 %collective-permute-start.15 = (bf16[128,1024]{1,0:T(8,128)(2,1)}, bf16[128,1024]{1,0:T(8,128)(2,1)}, u32[]{:S(2)}, u32[]{:S(2)}) collective-permute-start(bf16[128,1024]{1,0:T(8,128)(2,1)} %fusion.71), channel_id=1, source_target_pairs={{0,7},{1,0},{2,1},{3,2},{4,3},{5,4},{6,5},{7,6},{8,15},{9,8},{10,9... | collective-permute-start | bytes 786440 | tf_op jit(solution)/shard_map/ppermute | solution.py:17
  211.8 2.8 %copy-start = (f32[128,8192]{1,0:T(8,128)S(1)}, f32[128,8192]{1,0:T(8,128)}, u32[]{:S(2)}) copy-start(f32[128,8192]{1,0:T(8,128)} %copy.119) | copy-start | bytes 12582916
  211.9 11.2 %collective-permute-start.11 = (bf16[128,1024]{1,0:T(8,128)(2,1)S(1)}, bf16[128,1024]{1,0:T(8,128)(2,1)}, u32[]{:S(2)}, u32[]{:S(2)}) collective-permute-start(bf16[128,1024]{1,0:T(8,128)(2,1)S(1)} %fusion.75), channel_id=1, source_target_pairs={{0,7},{1,0},{2,1},{3,2},{4,3},{5,4},{6,5},{7,6},{8,15},{9,8},{10,9... | collective-permute-start | bytes 786440 | tf_op jit(solution)/shard_map/ppermute | solution.py:17
  214.6 3.9 %copy-start.2 = (bf16[8,128,8,128]{1,3,2,0:T(8,128)(2,1)S(1)}, bf16[8,128,8,128]{1,3,2,0:T(8,128)(2,1)}, u32[]{:S(2)}) copy-start(bf16[8,128,8,128]{1,3,2,0:T(8,128)(2,1)} %get-tuple-element.110) | copy-start | bytes 6291460
  (1 other events, 1.1 us)
where the time goes:
time: 227 us; the launch traced here: 225 us
  matrix products  81.1 us (36%)
  local copies, waits for them, and re-layouts  65.4 us (29%)
  other arithmetic  40.2 us (18%)
  starting transfers between devices  32.4 us (14%)
  waiting for transfers between devices  4.17 us (2%)
    unnamed x45, local copies, waits for them, and re-layouts  35.5 us
    ppermute x8, starting transfers between devices, passed_along_2(): lax.ppermute(value, axis, [(source, source + steps) for source in range(l...  21 us
    dot_general x8, matrix products, per_group(): jnp.einsum('grc,cd->rgd', weights.astype(jnp.bfloat16), value_group, pref...  20.3 us
    dot_general x8, matrix products, per_group(): jnp.einsum('grc,rgd->cd', probs.astype(jnp.bfloat16), grad_group, preferr...  18 us
    dot_general x8, matrix products, per_group(): jnp.einsum('rgd,cd->grc', grad_group, value_group, preferred_element_type...  15.6 us
    ppermute x8, starting transfers between devices, passed_along(): return lax.ppermute(value, axis, pairs)  11.4 us
    another operation x2, local copies, waits for them, and re-layouts, body(): part_rows.reshape(row_count, QUERY_HEADS, HEAD_SIZE)  11.1 us
    and x16, other arithmetic, allowed_pairs(): same_doc & causal & within & query_usable[:, None] & key_usable[None, :]  11 us
  transfers between devices with their start and end apart: 16, of which 3 were waited for; matrix products, arithmetic and copies ran while one was open for 26% of the time, Pallas kernels for 0%

commit v1 on v0

v1 whole, which is shorter than its diff:
```python
import functools

import jax
import jax.numpy as jnp
from jax import lax
from jax.experimental import pallas as pl
from jax.experimental.pallas import tpu as pltpu
from jax.sharding import PartitionSpec as P

KEY_VALUE_HEADS = 8
GROUP = 8
HEAD_SIZE = 128
BLOCK = 128
WIDE = GROUP * HEAD_SIZE
NEG = -1e30
SCALING = HEAD_SIZE**-0.5
LOG2E = 1.4426950408889634
PAIR = 2
AHEAD = 3
MESH = pl.DeviceIdType.MESH

NT = (((1,), (1,)), ((), ()))


def dot(a, b):
    return jnp.dot(a, b, preferred_element_type=jnp.float32)


def columns(head, width):
    return pl.ds(pl.multiple_of(head * width, width), width)


def kernel(
    outer_count,
    inner_count,
    q_hbm,
    k_hbm,
    v_hbm,
    g_hbm,
    doc_hbm,
    att_hbm,
    dq_hbm,
    dk_hbm,
    dv_hbm,
    q,
    g,
    docs,
    bias,
    kv,
    part,
    far_out,
    far_in,
    sum_out,
    sum_in,
    att,
    dq,
    dkv,
    in_sem,
    own_sem,
    doc_sem,
    own_send,
    near_recv,
    fwd_send,
    far_recv,
    back_send,
    back_recv,
    sum_send,
    sum_recv,
    out_sem,
    dkv_sem,
):
    place = lax.axis_index("outer") * inner_count + lax.axis_index("inner")
    total = outer_count * inner_count
    after = lax.rem(place + 1, total)
    before = lax.rem(place + total - 1, total)
    next_id = (after // inner_count, lax.rem(after, inner_count))
    prev_id = (before // inner_count, lax.rem(before, inner_count))

    def remote(src, dst, send, recv, device):
        return pltpu.make_async_remote_copy(
            src_ref=src,
            dst_ref=dst,
            send_sem=send,
            recv_sem=recv,
            device_id=device,
            device_id_type=MESH,
        )

    def own_copy(h, which):
        source = (k_hbm, v_hbm)[which]
        return remote(
            source.at[:, columns(h, HEAD_SIZE)],
            kv.at[h, which, 1],
            own_send.at[h, which],
            near_recv.at[h, which],
            next_id,
        )

    def forward_copy(h):
        return remote(kv.at[h, :, 1], kv.at[h, :, 2], fwd_send.at[h], far_recv.at[h], next_id)

    def back_copy(h, which):
        return remote(
            far_out.at[h, which],
            far_in.at[h, which],
            back_send.at[h, which],
            back_recv.at[h, which],
            prev_id,
        )

    def sum_copy(h):
        return remote(sum_out.at[h], sum_in.at[h], sum_send.at[h], sum_recv.at[h], prev_id)

    def load_copies(h):
        wide = columns(h, WIDE)
        narrow = columns(h, HEAD_SIZE)
        return (
            pltpu.make_async_copy(q_hbm.at[:, wide], q.at[:, wide], in_sem.at[h, 0]),
            pltpu.make_async_copy(g_hbm.at[:, wide], g.at[:, wide], in_sem.at[h, 1]),
            pltpu.make_async_copy(k_hbm.at[:, narrow], kv.at[h, 0, 0], own_sem.at[h, 0]),
            pltpu.make_async_copy(v_hbm.at[:, narrow], kv.at[h, 1, 0], own_sem.at[h, 1]),
        )

    def store_copies(h):
        wide = columns(h, WIDE)
        return (
            pltpu.make_async_copy(att.at[:, wide], att_hbm.at[:, wide], out_sem.at[h, 0]),
            pltpu.make_async_copy(dq.at[:, wide], dq_hbm.at[:, wide], out_sem.at[h, 1]),
        )

    def grad_copies(h):
        narrow = columns(h, HEAD_SIZE)
        return (
            pltpu.make_async_copy(dkv.at[h, 0], dk_hbm.at[:, narrow], dkv_sem.at[h, 0]),
            pltpu.make_async_copy(dkv.at[h, 1], dv_hbm.at[:, narrow], dkv_sem.at[h, 1]),
        )

    doc_copy = pltpu.make_async_copy(doc_hbm, docs, doc_sem)
    doc_copy.start()

    barrier = pltpu.get_barrier_semaphore()
    for neighbour in (prev_id, next_id):
        pl.semaphore_signal(barrier, inc=1, device_id=neighbour, device_id_type=MESH)
    pl.semaphore_wait(barrier, 2)

    for h in range(AHEAD):
        own_copy(h, 0).start()
        own_copy(h, 1).start()

    def start_loads(h, carry):
        for copy in load_copies(h):
            copy.start()
        return carry

    lax.fori_loop(0, KEY_VALUE_HEADS, start_loads, 0)

    doc_copy.wait()
    own_labels = docs[pl.ds(place, 1), :]
    query_labels = jnp.broadcast_to(own_labels, (BLOCK, BLOCK))
    for which in range(3):
        row = docs[pl.ds(jnp.maximum(place - which, 0), 1), :]
        key_labels = jnp.broadcast_to(row, (BLOCK, BLOCK)).T
        allowed = key_labels == query_labels
        if which == 0:
            key_place = lax.broadcasted_iota(jnp.int32, (BLOCK, BLOCK), 0)
            query_place = lax.broadcasted_iota(jnp.int32, (BLOCK, BLOCK), 1)
            allowed = allowed & (key_place <= query_place)
        else:
            allowed = allowed & jnp.broadcast_to(place >= which, (BLOCK, BLOCK))
        bias[pl.ds(which * BLOCK, BLOCK), :] = jnp.where(allowed, 0.0, NEG)

    def pass_on(h):
        own_copy(h, 0).wait_recv()
        own_copy(h, 1).wait_recv()
        forward_copy(h).start()

    def combine(h):
        back_copy(h, 0).wait_recv()
        back_copy(h, 1).wait_recv()
        sum_out[h] = (part[h, :, 1] + far_in[h].astype(jnp.float32)).astype(jnp.bfloat16)
        sum_copy(h).start()

    def finish(h):
        sum_copy(h).wait_recv()
        dkv[h] = (part[h, :, 0] + sum_in[h].astype(jnp.float32)).astype(jnp.bfloat16)
        for copy in grad_copies(h):
            copy.start()

    def attend(h):
        keys = kv[h, 0].reshape(3 * BLOCK, HEAD_SIZE)
        values = kv[h, 1].reshape(3 * BLOCK, HEAD_SIZE)
        keys_t = keys.T
        values_t = values.T
        masked = bias[...]
        masked = jnp.concatenate([masked] * PAIR, axis=1)
        queries, grads, probs_all, scores_all = [], [], [], []
        for group in range(0, GROUP, PAIR):

            def rows(ref):
                return jnp.concatenate(
                    [ref[:, columns(h * GROUP + group + n, HEAD_SIZE)] for n in range(PAIR)],
                    axis=0,
                )

            query, grad = rows(q), rows(g)
            scores = lax.dot_general(keys, query, NT, preferred_element_type=jnp.float32)
            scores = scores * (SCALING * LOG2E) + masked
            top = jnp.max(scores, axis=0, keepdims=True)
            weights = jnp.exp2(scores - top)
            sums = jnp.sum(weights, axis=0, keepdims=True)
            probs = weights * (1.0 / sums)
            coarse = probs.astype(jnp.bfloat16)
            grad_weights = lax.dot_general(values, grad, NT, preferred_element_type=jnp.float32)
            products = probs * grad_weights
            row_dot = jnp.sum(products, axis=0, keepdims=True)
            grad_scores = (products - probs * row_dot).astype(jnp.bfloat16)
            attended = dot(values_t, coarse).astype(jnp.bfloat16)
            query_grad = (dot(keys_t, grad_scores) * SCALING).astype(jnp.bfloat16)
            for n in range(PAIR):
                place_of = columns(h * GROUP + group + n, HEAD_SIZE)
                att[:, place_of] = attended[:, n * BLOCK : (n + 1) * BLOCK].T
                dq[:, place_of] = query_grad[:, n * BLOCK : (n + 1) * BLOCK].T
            queries.append(query)
            grads.append(grad)
            probs_all.append(coarse)
            scores_all.append(grad_scores)
        grad_rows = jnp.concatenate(grads, axis=0)
        query_rows = jnp.concatenate(queries, axis=0)
        value_part = dot(jnp.concatenate(probs_all, axis=1), grad_rows)
        key_part = dot(jnp.concatenate(scores_all, axis=1), query_rows) * SCALING
        for which, value in ((0, key_part), (1, value_part)):
            far_out[h, which] = value[2 * BLOCK :].astype(jnp.bfloat16)
            part[h, which] = value[: 2 * BLOCK].reshape(2, BLOCK, HEAD_SIZE)
            back_copy(h, which).start()
        for copy in store_copies(h):
            copy.start()

    pass_on(0)

    def step(h, carry):
        @pl.when(h + 1 < KEY_VALUE_HEADS)
        def _():
            pass_on(h + 1)

        @pl.when(h + AHEAD < KEY_VALUE_HEADS)
        def _():
            own_copy(h + AHEAD, 0).start()
            own_copy(h + AHEAD, 1).start()

        for copy in load_copies(h):
            copy.wait()
        forward_copy(h).wait_recv()
        attend(h)

        @pl.when(h >= 1)
        def _():
            combine(h - 1)

        @pl.when(h >= 2)
        def _():
            finish(h - 2)

        return carry

    lax.fori_loop(0, KEY_VALUE_HEADS, step, 0)
    last = KEY_VALUE_HEADS - 1
    combine(last)
    finish(last - 1)
    finish(last)

    def drain(h, carry):
        own_copy(h, 0).wait_send()
        own_copy(h, 1).wait_send()
        forward_copy(h).wait_send()
        back_copy(h, 0).wait_send()
        back_copy(h, 1).wait_send()
        sum_copy(h).wait_send()
        for copy in store_copies(h):
            copy.wait()
        for copy in grad_copies(h):
            copy.wait()
        return carry

    lax.fori_loop(0, KEY_VALUE_HEADS, drain, 0)


def body(outer_count, inner_count, query_matrix, key_matrix, value_matrix, output_gradient, doc_ids):
    heads = KEY_VALUE_HEADS
    any_spec = pl.BlockSpec(memory_space=pl.ANY)
    labels = doc_ids.reshape(doc_ids.shape[0] // BLOCK, BLOCK)
    tile = (BLOCK, HEAD_SIZE)
    bf16, f32 = jnp.bfloat16, jnp.float32
    dma = pltpu.SemaphoreType.DMA
    return pl.pallas_call(
        functools.partial(kernel, outer_count, inner_count),
        out_shape=(
            jax.ShapeDtypeStruct(query_matrix.shape, bf16),
            jax.ShapeDtypeStruct(query_matrix.shape, bf16),
            jax.ShapeDtypeStruct(key_matrix.shape, bf16),
            jax.ShapeDtypeStruct(value_matrix.shape, bf16),
        ),
        in_specs=[any_spec] * 5,
        out_specs=(any_spec,) * 4,
        scratch_shapes=[
            pltpu.VMEM(query_matrix.shape, bf16),
            pltpu.VMEM(query_matrix.shape, bf16),
            pltpu.VMEM(labels.shape, jnp.int32),
            pltpu.VMEM((3 * BLOCK, BLOCK), f32),
            pltpu.VMEM((heads, 2, 3) + tile, bf16),
            pltpu.VMEM((heads, 2, 2) + tile, f32),
            pltpu.VMEM((heads, 2) + tile, bf16),
            pltpu.VMEM((heads, 2) + tile, bf16),
            pltpu.VMEM((heads, 2) + tile, bf16),
            pltpu.VMEM((heads, 2) + tile, bf16),
            pltpu.VMEM(query_matrix.shape, bf16),
            pltpu.VMEM(query_matrix.shape, bf16),
            pltpu.VMEM((heads, 2) + tile, bf16),
            dma((heads, 2)),
            dma((heads, 2)),
            dma(()),
            dma((heads, 2)),
            dma((heads, 2)),
            dma((heads,)),
            dma((heads,)),
            dma((heads, 2)),
            dma((heads, 2)),
            dma((heads,)),
            dma((heads,)),
            dma((heads, 2)),
            dma((heads, 2)),
        ],
        compiler_params=pltpu.CompilerParams(
            collective_id=0, has_side_effects=True, vmem_limit_bytes=48 * 1024 * 1024
        ),
    )(query_matrix, key_matrix, value_matrix, output_gradient, labels)


def solution(mesh):
    split = P(("outer", "inner"), None)
    return jax.shard_map(
        functools.partial(body, mesh.shape["outer"], mesh.shape["inner"]),
        mesh=mesh,
        in_specs=(split, split, split, split, P()),
        out_specs=(split, split, split, split),
        check_vma=False,
    )
```

time: 227 us -> 63 us (0.28)
  the two profiles are of different devices: /device:TPU:24 before, /device:TPU:223 now
where the time goes in v1:
time: 63 us; the launch traced here: 62.8 us
  Pallas kernels  55.4 us (88%)
  local copies, waits for them, and re-layouts  6.84 us (11%)
  between operations  0.65 us (1%)
    pallas_call x1, Pallas kernels, body(): pl.pallas_call(functools.partial(kernel, outer_count, inner_count), out_s...  55.4 us
    unnamed x10, local copies, waits for them, and re-layouts  6.84 us

profile of v1, /device:TPU:223, one launch (start us, length us, event | category | flops | bytes accessed | tf_op | source)
XLA Modules:
  0.0 62.8 jit_solution(13785042821081061451)
XLA Ops:
  0.6 0.0 copy-start
  0.6 0.9 %copy-done = bf16[128,1024]{1,0:T(8,128)(2,1)S(1)} copy-done((bf16[128,1024]{1,0:T(8,128)(2,1)S(1)}, bf16[128,1024]{1,0:T(8,128)(2,1)}, u32[]{:S(2)}) %copy-start) | copy-done | bytes 262168
  1.6 0.0 copy-start.1
  1.6 0.9 %copy-done.1 = bf16[128,1024]{1,0:T(8,128)(2,1)S(1)} copy-done((bf16[128,1024]{1,0:T(8,128)(2,1)S(1)}, bf16[128,1024]{1,0:T(8,128)(2,1)}, u32[]{:S(2)}) %copy-start.1) | copy-done | bytes 262168
  2.5 0.0 copy-start.2
  2.5 0.9 %copy-done.2 = s32[32768]{0:T(1024)S(1)} copy-done((s32[32768]{0:T(1024)S(1)}, s32[32768]{0:T(1024)}, u32[]{:S(2)}) %copy-start.2) | copy-done | bytes 131096
  3.4 55.4 %shard_map.84 = (bf16[128,8192]{1,0:T(8,128)(2,1)S(1)}, bf16[128,8192]{1,0:T(8,128)(2,1)S(1)}, bf16[128,1024]{1,0:T(8,128)(2,1)S(1)}, bf16[128,1024]{1,0:T(8,128)(2,1)S(1)}) custom-call(bf16[128,8192]{1,0:T(8,128)(2,1)} %q_hbm.1, bf16[128,1024]{1,0:T(8,128)(2,1)S(1)} %copy-done, bf16[128,1024]{1,0:T(8,128)(2,1)S(1)} %copy-done.1, bf16[128,8192]{1,0:T(8,128)(2,1)} %g_hbm.1, ...), custom_call_target="tpu_custom_call" | custom-call | tf_op jit(solution)/shard_map/pallas_call | solution.py:294
  58.8 1.3 %copy.13 = bf16[128,8192]{1,0:T(8,128)(2,1)} copy(bf16[128,8192]{1,0:T(8,128)(2,1)S(1)} %get-tuple-element.8) | data formatting | bytes 4194304
  60.1 1.3 %copy.14 = bf16[128,8192]{1,0:T(8,128)(2,1)} copy(bf16[128,8192]{1,0:T(8,128)(2,1)S(1)} %get-tuple-element.9) | data formatting | bytes 4194304
  61.4 0.7 %copy.15 = bf16[128,1024]{1,0:T(8,128)(2,1)} copy(bf16[128,1024]{1,0:T(8,128)(2,1)S(1)} %get-tuple-element.10) | data formatting | bytes 524288
  62.1 0.7 %copy.16 = bf16[128,1024]{1,0:T(8,128)(2,1)} copy(bf16[128,1024]{1,0:T(8,128)(2,1)S(1)} %get-tuple-element.11) | data formatting | bytes 524288
Async XLA Ops:
  0.6 1.0 %copy-start = (bf16[128,1024]{1,0:T(8,128)(2,1)S(1)}, bf16[128,1024]{1,0:T(8,128)(2,1)}, u32[]{:S(2)}) copy-start(bf16[128,1024]{1,0:T(8,128)(2,1)} %k_hbm.1) | copy-start | bytes 786436
  1.6 0.9 %copy-start.1 = (bf16[128,1024]{1,0:T(8,128)(2,1)S(1)}, bf16[128,1024]{1,0:T(8,128)(2,1)}, u32[]{:S(2)}) copy-start(bf16[128,1024]{1,0:T(8,128)(2,1)} %v_hbm.1) | copy-start | bytes 786436
  2.5 0.9 %copy-start.2 = (s32[32768]{0:T(1024)S(1)}, s32[32768]{0:T(1024)}, u32[]{:S(2)}) copy-start(s32[32768]{0:T(1024)} %param.9) | copy-start | bytes 393220

commit v2 on v1

v2 whole, which is shorter than its diff:
```python
import functools

import jax
import jax.numpy as jnp
from jax import lax
from jax.experimental import pallas as pl
from jax.experimental.pallas import tpu as pltpu
from jax.sharding import PartitionSpec as P

HEADS = 8
GROUP = 8
HEAD_SIZE = 128
BLOCK = 128
WIDE = GROUP * HEAD_SIZE
NEG = -1e30
SCALING = HEAD_SIZE**-0.5
LOG2E = 1.4426950408889634
MESH = pl.DeviceIdType.MESH
BOTH = (0, 1)

NT = (((1,), (1,)), ((), ()))
TN = (((0,), (0,)), ((), ()))


def dot(a, b):
    return jnp.dot(a, b, preferred_element_type=jnp.float32)


def dot_of(a, b, dims):
    return lax.dot_general(a, b, dims, preferred_element_type=jnp.float32)


def columns(head, width):
    return pl.ds(pl.multiple_of(head * width, width), width)


def kernel(
    outer_count,
    inner_count,
    q_hbm,
    k_hbm,
    v_hbm,
    g_hbm,
    doc_hbm,
    att,
    dq,
    dk,
    dv,
    q,
    g,
    docs,
    bias,
    kv,
    part,
    far_out,
    far_in,
    sum_out,
    sum_in,
    in_sem,
    own_sem,
    doc_sem,
    own_send,
    near_recv,
    fwd_send,
    far_recv,
    back_send,
    back_recv,
    sum_send,
    sum_recv,
):
    place = lax.axis_index("outer") * inner_count + lax.axis_index("inner")
    total = outer_count * inner_count
    has_prev = place >= 1
    has_prev2 = place >= 2
    has_next = place <= total - 2
    has_both = has_prev & has_next
    after = jnp.minimum(place + 1, total - 1)
    before = jnp.maximum(place - 1, 0)
    next_id = (after // inner_count, lax.rem(after, inner_count))
    prev_id = (before // inner_count, lax.rem(before, inner_count))

    def remote(src, dst, send, recv, device):
        return pltpu.make_async_remote_copy(
            src_ref=src,
            dst_ref=dst,
            send_sem=send,
            recv_sem=recv,
            device_id=device,
            device_id_type=MESH,
        )

    def own_copy(h, which):
        source = (k_hbm, v_hbm)[which]
        return remote(
            source.at[:, columns(h, HEAD_SIZE)],
            kv.at[h, which, 1],
            own_send.at[h, which],
            near_recv.at[h, which],
            next_id,
        )

    def forward_copy(h, which):
        return remote(
            kv.at[h, which, 1],
            kv.at[h, which, 2],
            fwd_send.at[h, which],
            far_recv.at[h, which],
            next_id,
        )

    def back_copy(h, which):
        return remote(
            far_out.at[h, which],
            far_in.at[h, which],
            back_send.at[h, which],
            back_recv.at[h, which],
            prev_id,
        )

    def sum_copy(h, which):
        return remote(
            sum_out.at[h, which],
            sum_in.at[h, which],
            sum_send.at[h, which],
            sum_recv.at[h, which],
            prev_id,
        )

    def load_copies(h):
        wide = columns(h, WIDE)
        narrow = columns(h, HEAD_SIZE)
        return (
            pltpu.make_async_copy(q_hbm.at[:, wide], q.at[:, wide], in_sem.at[h, 0]),
            pltpu.make_async_copy(g_hbm.at[:, wide], g.at[:, wide], in_sem.at[h, 1]),
            pltpu.make_async_copy(k_hbm.at[:, narrow], kv.at[h, 0, 0], own_sem.at[h, 0]),
            pltpu.make_async_copy(v_hbm.at[:, narrow], kv.at[h, 1, 0], own_sem.at[h, 1]),
        )

    doc_copy = pltpu.make_async_copy(doc_hbm, docs, doc_sem)
    doc_copy.start()

    barrier = pltpu.get_barrier_semaphore()

    @pl.when(has_prev)
    def _():
        pl.semaphore_signal(barrier, inc=1, device_id=prev_id, device_id_type=MESH)

    @pl.when(has_next)
    def _():
        pl.semaphore_signal(barrier, inc=1, device_id=next_id, device_id_type=MESH)

    pl.semaphore_wait(barrier, jnp.where(has_both, 2, 1))

    def send_own(h):
        @pl.when(has_next)
        def _():
            for which in BOTH:
                own_copy(h, which).start()

    def pass_on(h):
        @pl.when(has_prev)
        def _():
            for which in BOTH:
                own_copy(h, which).wait_recv()

                @pl.when(has_next)
                def _():
                    forward_copy(h, which).start()

    send_own(0)
    send_own(1)

    def start_loads(h, carry):
        for copy in load_copies(h):
            copy.start()
        return carry

    lax.fori_loop(0, HEADS, start_loads, 0)

    @pl.when(place <= 1)
    def _():
        blank = jnp.zeros((HEADS, 2, BLOCK, HEAD_SIZE), jnp.bfloat16)
        kv[:, :, 2] = blank

        @pl.when(place == 0)
        def _():
            kv[:, :, 1] = blank

    @pl.when(place == total - 1)
    def _():
        far_in[...] = jnp.zeros_like(far_in)
        sum_in[...] = jnp.zeros_like(sum_in)

    doc_copy.wait()
    own_labels = jnp.broadcast_to(docs[pl.ds(place, 1), :], (BLOCK, BLOCK)).T
    for which in range(3):
        row = docs[pl.ds(jnp.maximum(place - which, 0), 1), :]
        allowed = jnp.broadcast_to(row, (BLOCK, BLOCK)) == own_labels
        if which == 0:
            query_place = lax.broadcasted_iota(jnp.int32, (BLOCK, BLOCK), 0)
            key_place = lax.broadcasted_iota(jnp.int32, (BLOCK, BLOCK), 1)
            allowed = allowed & (key_place <= query_place)
        else:
            allowed = allowed & jnp.broadcast_to(place >= which, (BLOCK, BLOCK))
        bias[:, which * BLOCK : (which + 1) * BLOCK] = jnp.where(allowed, 0.0, NEG)

    def combine(h):
        @pl.when(has_prev)
        def _():
            for which in (1, 0):

                @pl.when(has_next)
                def _():
                    back_copy(h, which).wait_recv()

                sum_out[h, which] = (
                    part[h, which, 1] + far_in[h, which].astype(jnp.float32)
                ).astype(jnp.bfloat16)
                sum_copy(h, which).start()

    def finish(h):
        for which in (1, 0):

            @pl.when(has_next)
            def _():
                sum_copy(h, which).wait_recv()

            (dk, dv)[which][:, columns(h, HEAD_SIZE)] = (
                part[h, which, 0] + sum_in[h, which].astype(jnp.float32)
            ).astype(jnp.bfloat16)

    def attend(h):
        keys = kv[h, 0].reshape(3 * BLOCK, HEAD_SIZE)
        values = kv[h, 1].reshape(3 * BLOCK, HEAD_SIZE)

        def rows(ref):
            return jnp.concatenate(
                [ref[:, columns(h * GROUP + n, HEAD_SIZE)] for n in range(GROUP)], axis=0
            )

        query, grad = rows(q), rows(g)
        scores = dot_of(query, keys, NT)
        grad_weights = dot_of(grad, values, NT)
        scores = scores * (SCALING * LOG2E) + jnp.concatenate([bias[...]] * GROUP, axis=0)
        top = jnp.max(scores, axis=1, keepdims=True)
        weights = jnp.exp2(scores - top)
        sums = jnp.sum(weights, axis=1, keepdims=True)
        probs = weights * (1.0 / sums)
        coarse = probs.astype(jnp.bfloat16)
        products = probs * grad_weights
        row_dot = jnp.sum(products, axis=1, keepdims=True)
        grad_scores = (products - probs * row_dot).astype(jnp.bfloat16)
        far_out[h, 1] = dot_of(coarse[:, 2 * BLOCK :], grad, TN).astype(jnp.bfloat16)
        far_out[h, 0] = (dot_of(grad_scores[:, 2 * BLOCK :], query, TN) * SCALING).astype(
            jnp.bfloat16
        )

        @pl.when(has_prev2)
        def _():
            for which in (1, 0):
                back_copy(h, which).start()

        value_part = dot_of(coarse[:, : 2 * BLOCK], grad, TN)
        key_part = dot_of(grad_scores[:, : 2 * BLOCK], query, TN) * SCALING
        for which, value in ((0, key_part), (1, value_part)):
            part[h, which] = value.reshape(2, BLOCK, HEAD_SIZE)
        attended = dot(coarse, values).astype(jnp.bfloat16)
        query_grad = (dot(grad_scores, keys) * SCALING).astype(jnp.bfloat16)
        for n in range(GROUP):
            place_of = columns(h * GROUP + n, HEAD_SIZE)
            att[:, place_of] = attended[n * BLOCK : (n + 1) * BLOCK]
            dq[:, place_of] = query_grad[n * BLOCK : (n + 1) * BLOCK]

    pass_on(0)
    send_own(2)
    pass_on(1)
    send_own(3)

    def step(h, carry):
        for copy in load_copies(h):
            copy.wait()

        @pl.when(has_prev2)
        def _():
            for which in BOTH:
                forward_copy(h, which).wait_recv()

        attend(h)

        @pl.when(h + 2 < HEADS)
        def _():
            pass_on(h + 2)

        @pl.when(h + 4 < HEADS)
        def _():
            send_own(h + 4)

        @pl.when(h >= 1)
        def _():
            combine(h - 1)

        @pl.when(h >= 3)
        def _():
            finish(h - 3)

        return carry

    lax.fori_loop(0, HEADS, step, 0)
    combine(HEADS - 1)
    for late in (3, 2, 1):
        finish(HEADS - late)

    def drain(h, carry):
        for which in BOTH:

            @pl.when(has_next)
            def _():
                own_copy(h, which).wait_send()

            @pl.when(has_both)
            def _():
                forward_copy(h, which).wait_send()

            @pl.when(has_prev2)
            def _():
                back_copy(h, which).wait_send()

            @pl.when(has_prev)
            def _():
                sum_copy(h, which).wait_send()

        return carry

    lax.fori_loop(0, HEADS, drain, 0)


def store_kernel(*refs):
    sources, targets, sems = refs[:4], refs[4:8], refs[8]
    copies = [
        pltpu.make_async_copy(source, target, sems.at[n])
        for n, (source, target) in enumerate(zip(sources, targets))
    ]
    for copy in copies:
        copy.start()
    for copy in copies:
        copy.wait()


def body(outer_count, inner_count, query_matrix, key_matrix, value_matrix, output_gradient, doc_ids):
    hbm = pl.BlockSpec(memory_space=pltpu.HBM)
    vmem = pl.BlockSpec(memory_space=pltpu.VMEM)
    labels = doc_ids.reshape(doc_ids.shape[0] // BLOCK, BLOCK)
    tile = (BLOCK, HEAD_SIZE)
    bf16, f32 = jnp.bfloat16, jnp.float32
    dma = pltpu.SemaphoreType.DMA
    shapes = [query_matrix.shape, query_matrix.shape, key_matrix.shape, value_matrix.shape]
    operands = [
        pltpu.with_memory_space_constraint(operand, pltpu.HBM)
        for operand in (query_matrix, key_matrix, value_matrix, output_gradient, labels)
    ]
    results = pl.pallas_call(
        functools.partial(kernel, outer_count, inner_count),
        out_shape=[pltpu.VMEM(shape, bf16) for shape in shapes],
        in_specs=[hbm] * 5,
        out_specs=[vmem] * 4,
        scratch_shapes=[
            pltpu.VMEM(query_matrix.shape, bf16),
            pltpu.VMEM(query_matrix.shape, bf16),
            pltpu.VMEM(labels.shape, jnp.int32),
            pltpu.VMEM((BLOCK, 3 * BLOCK), f32),
            pltpu.VMEM((HEADS, 2, 3) + tile, bf16),
            pltpu.VMEM((HEADS, 2, 2) + tile, f32),
        ]
        + [pltpu.VMEM((HEADS, 2) + tile, bf16)] * 4
        + [dma((HEADS, 2)), dma((HEADS, 2)), dma(())]
        + [dma((HEADS, 2))] * 8,
        compiler_params=pltpu.CompilerParams(
            collective_id=0, has_side_effects=True, vmem_limit_bytes=44 * 1024 * 1024
        ),
    )(*operands)
    results = [pltpu.with_memory_space_constraint(result, pltpu.VMEM) for result in results]
    return pl.pallas_call(
        store_kernel,
        out_shape=[jax.ShapeDtypeStruct(shape, bf16) for shape in shapes],
        in_specs=[vmem] * 4,
        out_specs=[pl.BlockSpec(memory_space=pltpu.HBM)] * 4,
        scratch_shapes=[dma((4,))],
        compiler_params=pltpu.CompilerParams(vmem_limit_bytes=1024 * 1024),
    )(*results)


def solution(mesh):
    split = P(("outer", "inner"), None)
    return jax.shard_map(
        functools.partial(body, mesh.shape["outer"], mesh.shape["inner"]),
        mesh=mesh,
        in_specs=(split, split, split, split, P()),
        out_specs=(split, split, split, split),
        check_vma=False,
    )
```

time: 63 us -> 46.8 us (0.74)
  the two profiles are of different devices: /device:TPU:223 before, /device:TPU:24 now
where the time goes in v2:
time: 46.8 us; the launch traced here: 46.7 us
  Pallas kernels  46.1 us (99%)
  between operations  0.64 us (1%)
    pallas_call x1, Pallas kernels, body(): pl.pallas_call(functools.partial(kernel, outer_count, inner_count), out_s...  43.9 us
    pallas_call x1, Pallas kernels, body(): pl.pallas_call(store_kernel, out_shape=[jax.ShapeDtypeStruct(shape, bf16)...  2.2 us

profile of v2, /device:TPU:24, one launch (start us, length us, event | category | flops | bytes accessed | tf_op | source)
XLA Modules:
  0.0 46.7 jit_solution(16720546146983257714)
XLA Ops:
  0.6 43.9 %shard_map.84 = (bf16[128,8192]{1,0:T(8,128)(2,1)S(1)}, bf16[128,8192]{1,0:T(8,128)(2,1)S(1)}, bf16[128,1024]{1,0:T(8,128)(2,1)S(1)}, bf16[128,1024]{1,0:T(8,128)(2,1)S(1)}) custom-call(bf16[128,8192]{1,0:T(8,128)(2,1)} %q_hbm.1, bf16[128,1024]{1,0:T(8,128)(2,1)} %k_hbm.1, bf16[128,1024]{1,0:T(8,128)(2,1)} %v_hbm.1, bf16[128,8192]{1,0:T(8,128)(2,1)} %g_hbm.1, ...), custom_call_target="tpu_custom_call" | custom-call | tf_op jit(solution)/shard_map/pallas_call | solution.py:361
  44.5 2.2 %shard_map.85 = (bf16[128,8192]{1,0:T(8,128)(2,1)}, bf16[128,8192]{1,0:T(8,128)(2,1)}, bf16[128,1024]{1,0:T(8,128)(2,1)}, bf16[128,1024]{1,0:T(8,128)(2,1)}) custom-call(bf16[128,8192]{1,0:T(8,128)(2,1)S(1)} %get-tuple-element.8.refs_0_, bf16[128,8192]{1,0:T(8,128)(2,1)S(1)} %get-tuple-element.9.refs_1_, bf16[128,1024]{1,0:T(8,128)(2,1)S(1)} %get-tuple-element.10.refs_2_, ...), custom_call_target="tpu_custom_call" | custom-call | tf_op jit(solution)/shard_map/pallas_call | solution.py:382

commit v3 on v2

--- a/solution.py
+++ b/solution.py
@@ -17,6 +17,14 @@
 LOG2E = 1.4426950408889634
 MESH = pl.DeviceIdType.MESH
 BOTH = (0, 1)
+INIT = 2
+LEAD = 2
+LAG = 2
+FINAL = 4
+LOADS = 2
+EXTRA = 2
+EARLY = 1
+SPLIT = 2
 
 NT = (((1,), (1,)), ((), ()))
 TN = (((0,), (0,)), ((), ()))
@@ -147,9 +155,9 @@
 
     @pl.when(has_next)
     def _():
-        pl.semaphore_signal(barrier, inc=1, device_id=next_id, device_id_type=MESH)
-
-    pl.semaphore_wait(barrier, jnp.where(has_both, 2, 1))
+        pl.semaphore_wait(barrier, 1)
+
+    lead_in = INIT + jnp.where(lax.axis_index("inner") < EARLY, EXTRA, 0)
 
     def send_own(h):
         @pl.when(has_next)
@@ -167,15 +175,18 @@
                 def _():
                     forward_copy(h, which).start()
 
-    send_own(0)
-    send_own(1)
+    def start_own(h, carry):
+        send_own(h)
+        return carry
+
+    lax.fori_loop(0, lead_in, start_own, 0)
 
     def start_loads(h, carry):
         for copy in load_copies(h):
             copy.start()
         return carry
 
-    lax.fori_loop(0, HEADS, start_loads, 0)
+    lax.fori_loop(0, LOADS, start_loads, 0)
 
     @pl.when(place <= 1)
     def _():
@@ -229,9 +240,30 @@
                 part[h, which, 0] + sum_in[h, which].astype(jnp.float32)
             ).astype(jnp.bfloat16)
 
+    def next_own(h):
+        @pl.when(h + LEAD + lead_in < HEADS)
+        def _():
+            send_own(h + LEAD + lead_in)
+
+    def go_on(h):
+        @pl.when(h + LEAD < HEADS)
+        def _():
+            pass_on(h + LEAD)
+
+        next_own(h)
+
+    def wait_far(h):
+        @pl.when(has_prev2)
+        def _():
+            for which in BOTH:
+                forward_copy(h, which).wait_recv()
+
+    def combine_late(h):
+        @pl.when(h >= LAG)
+        def _():
+            combine(h - LAG)
+
     def attend(h):
-        keys = kv[h, 0].reshape(3 * BLOCK, HEAD_SIZE)
-        values = kv[h, 1].reshape(3 * BLOCK, HEAD_SIZE)
 
         def rows(ref):
             return jnp.concatenate(
@@ -239,6 +271,8 @@
             )
 
         query, grad = rows(q), rows(g)
+        keys = kv[h, 0].reshape(3 * BLOCK, HEAD_SIZE)
+        values = kv[h, 1].reshape(3 * BLOCK, HEAD_SIZE)
         scores = dot_of(query, keys, NT)
         grad_weights = dot_of(grad, values, NT)
         scores = scores * (SCALING * LOG2E) + jnp.concatenate([bias[...]] * GROUP, axis=0)
@@ -260,6 +294,7 @@
             for which in (1, 0):
                 back_copy(h, which).start()
 
+        go_on(h)
         value_part = dot_of(coarse[:, : 2 * BLOCK], grad, TN)
         key_part = dot_of(grad_scores[:, : 2 * BLOCK], query, TN) * SCALING
         for which, value in ((0, key_part), (1, value_part)):
@@ -271,43 +306,33 @@
             att[:, place_of] = attended[n * BLOCK : (n + 1) * BLOCK]
             dq[:, place_of] = query_grad[n * BLOCK : (n + 1) * BLOCK]
 
-    pass_on(0)
-    send_own(2)
-    pass_on(1)
-    send_own(3)
+    for h in range(LEAD):
+        pass_on(h)
+        send_own(h + lead_in)
 
     def step(h, carry):
         for copy in load_copies(h):
             copy.wait()
 
-        @pl.when(has_prev2)
-        def _():
-            for which in BOTH:
-                forward_copy(h, which).wait_recv()
-
+        @pl.when(h + LOADS < HEADS)
+        def _():
+            start_loads(h + LOADS, 0)
+
+        wait_far(h)
         attend(h)
 
-        @pl.when(h + 2 < HEADS)
-        def _():
-            pass_on(h + 2)
-
-        @pl.when(h + 4 < HEADS)
-        def _():
-            send_own(h + 4)
-
-        @pl.when(h >= 1)
-        def _():
-            combine(h - 1)
-
-        @pl.when(h >= 3)
-        def _():
-            finish(h - 3)
+        combine_late(h)
+
+        @pl.when(h >= FINAL)
+        def _():
+            finish(h - FINAL)
 
         return carry
 
     lax.fori_loop(0, HEADS, step, 0)
-    combine(HEADS - 1)
-    for late in (3, 2, 1):
+    for late in range(LAG, 0, -1):
+        combine(HEADS - late)
+    for late in range(FINAL, 0, -1):
         finish(HEADS - late)
 
     def drain(h, carry):
@@ -336,9 +361,13 @@
 
 def store_kernel(*refs):
     sources, targets, sems = refs[:4], refs[4:8], refs[8]
+    rows = BLOCK // SPLIT
     copies = [
-        pltpu.make_async_copy(source, target, sems.at[n])
+        pltpu.make_async_copy(
+            source.at[pl.ds(m * rows, rows)], target.at[pl.ds(m * rows, rows)], sems.at[n, m]
+        )
         for n, (source, target) in enumerate(zip(sources, targets))
+        for m in range(SPLIT)
     ]
     for copy in copies:
         copy.start()
@@ -384,7 +413,7 @@
         out_shape=[jax.ShapeDtypeStruct(shape, bf16) for shape in shapes],
         in_specs=[vmem] * 4,
         out_specs=[pl.BlockSpec(memory_space=pltpu.HBM)] * 4,
-        scratch_shapes=[dma((4,))],
+        scratch_shapes=[dma((4, SPLIT))],
         compiler_params=pltpu.CompilerParams(vmem_limit_bytes=1024 * 1024),
     )(*results)
 

time: 46.8 us -> 45.6 us (0.974)
  Pallas kernels: 46.1 us -> 44.9 us
    pallas_call x1, Pallas kernels: 43.9 us -> 42.6 us  [body(): pl.pallas_call(functools.partial(kernel, outer_count, inner_count), out_s...]
where the time goes in v3:
time: 45.6 us; the launch traced here: 45.5 us
  Pallas kernels  44.9 us (98%)
  between operations  0.64 us (1%)
    pallas_call x1, Pallas kernels, body(): pl.pallas_call(functools.partial(kernel, outer_count, inner_count), out_s...  42.6 us
    pallas_call x1, Pallas kernels, body(): pl.pallas_call(store_kernel, out_shape=[jax.ShapeDtypeStruct(shape, bf16)...  2.23 us

profile of v3, /device:TPU:24, one launch (start us, length us, event | category | flops | bytes accessed | tf_op | source)
XLA Modules:
  0.0 45.5 jit_solution(3814126762103553514)
XLA Ops:
  0.6 42.6 %shard_map.84 = (bf16[128,8192]{1,0:T(8,128)(2,1)S(1)}, bf16[128,8192]{1,0:T(8,128)(2,1)S(1)}, bf16[128,1024]{1,0:T(8,128)(2,1)S(1)}, bf16[128,1024]{1,0:T(8,128)(2,1)S(1)}) custom-call(bf16[128,8192]{1,0:T(8,128)(2,1)} %q_hbm.1, bf16[128,1024]{1,0:T(8,128)(2,1)} %k_hbm.1, bf16[128,1024]{1,0:T(8,128)(2,1)} %v_hbm.1, bf16[128,8192]{1,0:T(8,128)(2,1)} %g_hbm.1, ...), custom_call_target="tpu_custom_call" | custom-call | tf_op jit(solution)/shard_map/pallas_call | solution.py:390
  43.3 2.2 %shard_map.85 = (bf16[128,8192]{1,0:T(8,128)(2,1)}, bf16[128,8192]{1,0:T(8,128)(2,1)}, bf16[128,1024]{1,0:T(8,128)(2,1)}, bf16[128,1024]{1,0:T(8,128)(2,1)}) custom-call(bf16[128,8192]{1,0:T(8,128)(2,1)S(1)} %get-tuple-element.8.refs_0_, bf16[128,8192]{1,0:T(8,128)(2,1)S(1)} %get-tuple-element.9.refs_1_, bf16[128,1024]{1,0:T(8,128)(2,1)S(1)} %get-tuple-element.10.refs_2_, ...), custom_call_target="tpu_custom_call" | custom-call | tf_op jit(solution)/shard_map/pallas_call | solution.py:411

commit v4 on v3

--- a/solution.py
+++ b/solution.py
@@ -330,12 +330,8 @@
         return carry
 
     lax.fori_loop(0, HEADS, step, 0)
-    for late in range(LAG, 0, -1):
-        combine(HEADS - late)
-    for late in range(FINAL, 0, -1):
-        finish(HEADS - late)
-
-    def drain(h, carry):
+
+    def drain_forward(h, carry):
         for which in BOTH:
 
             @pl.when(has_next)
@@ -346,6 +342,11 @@
             def _():
                 forward_copy(h, which).wait_send()
 
+        return carry
+
+    def drain_back(h, carry):
+        for which in BOTH:
+
             @pl.when(has_prev2)
             def _():
                 back_copy(h, which).wait_send()
@@ -356,7 +357,15 @@
 
         return carry
 
-    lax.fori_loop(0, HEADS, drain, 0)
+    for late in range(LAG, 1, -1):
+        combine(HEADS - late)
+    lax.fori_loop(0, HEADS, drain_forward, 0)
+    lax.fori_loop(0, HEADS - FINAL, drain_back, 0)
+    finish(HEADS - FINAL)
+    combine(HEADS - 1)
+    for late in range(FINAL - 1, 0, -1):
+        finish(HEADS - late)
+    lax.fori_loop(HEADS - FINAL, HEADS, drain_back, 0)
 
 
 def store_kernel(*refs):

time: 45.6 us -> 45.5 us (level)
  no operation moved by 1% of the time
where the time goes in v4:
time: 45.5 us; the launch traced here: 45.4 us
  Pallas kernels  44.8 us (98%)
  between operations  0.64 us (1%)
    pallas_call x1, Pallas kernels, body(): pl.pallas_call(functools.partial(kernel, outer_count, inner_count), out_s...  42.6 us
    pallas_call x1, Pallas kernels, body(): pl.pallas_call(store_kernel, out_shape=[jax.ShapeDtypeStruct(shape, bf16)...  2.23 us

profile of v4, /device:TPU:24, one launch (start us, length us, event | category | flops | bytes accessed | tf_op | source)
XLA Modules:
  0.0 45.4 jit_solution(14674228641170165756)
XLA Ops:
  0.6 42.6 %shard_map.84 = (bf16[128,8192]{1,0:T(8,128)(2,1)S(1)}, bf16[128,8192]{1,0:T(8,128)(2,1)S(1)}, bf16[128,1024]{1,0:T(8,128)(2,1)S(1)}, bf16[128,1024]{1,0:T(8,128)(2,1)S(1)}) custom-call(bf16[128,8192]{1,0:T(8,128)(2,1)} %q_hbm.1, bf16[128,1024]{1,0:T(8,128)(2,1)} %k_hbm.1, bf16[128,1024]{1,0:T(8,128)(2,1)} %v_hbm.1, bf16[128,8192]{1,0:T(8,128)(2,1)} %g_hbm.1, ...), custom_call_target="tpu_custom_call" | custom-call | tf_op jit(solution)/shard_map/pallas_call | solution.py:399
  43.2 2.2 %shard_map.85 = (bf16[128,8192]{1,0:T(8,128)(2,1)}, bf16[128,8192]{1,0:T(8,128)(2,1)}, bf16[128,1024]{1,0:T(8,128)(2,1)}, bf16[128,1024]{1,0:T(8,128)(2,1)}) custom-call(bf16[128,8192]{1,0:T(8,128)(2,1)S(1)} %get-tuple-element.8.refs_0_, bf16[128,8192]{1,0:T(8,128)(2,1)S(1)} %get-tuple-element.9.refs_1_, bf16[128,1024]{1,0:T(8,128)(2,1)S(1)} %get-tuple-element.10.refs_2_, ...), custom_call_target="tpu_custom_call" | custom-call | tf_op jit(solution)/shard_map/pallas_call | solution.py:420

commit v5 on v4

--- a/solution.py
+++ b/solution.py
@@ -252,11 +252,10 @@
 
         next_own(h)
 
-    def wait_far(h):
+    def wait_far(h, which):
         @pl.when(has_prev2)
         def _():
-            for which in BOTH:
-                forward_copy(h, which).wait_recv()
+            forward_copy(h, which).wait_recv()
 
     def combine_late(h):
         @pl.when(h >= LAG)
@@ -271,11 +270,13 @@
             )
 
         query, grad = rows(q), rows(g)
+        wait_far(h, 0)
         keys = kv[h, 0].reshape(3 * BLOCK, HEAD_SIZE)
+        scores = dot_of(query, keys, NT)
+        scores = scores * (SCALING * LOG2E) + jnp.concatenate([bias[...]] * GROUP, axis=0)
+        wait_far(h, 1)
         values = kv[h, 1].reshape(3 * BLOCK, HEAD_SIZE)
-        scores = dot_of(query, keys, NT)
         grad_weights = dot_of(grad, values, NT)
-        scores = scores * (SCALING * LOG2E) + jnp.concatenate([bias[...]] * GROUP, axis=0)
         top = jnp.max(scores, axis=1, keepdims=True)
         weights = jnp.exp2(scores - top)
         sums = jnp.sum(weights, axis=1, keepdims=True)
@@ -318,7 +319,6 @@
         def _():
             start_loads(h + LOADS, 0)
 
-        wait_far(h)
         attend(h)
 
         combine_late(h)

time: 45.5 us -> 45.5 us (level)
  no operation moved by 1% of the time
where the time goes in v5:
time: 45.5 us; the launch traced here: 45.4 us
  Pallas kernels  44.7 us (98%)
  between operations  0.64 us (1%)
    pallas_call x1, Pallas kernels, body(): pl.pallas_call(functools.partial(kernel, outer_count, inner_count), out_s...  42.5 us
    pallas_call x1, Pallas kernels, body(): pl.pallas_call(store_kernel, out_shape=[jax.ShapeDtypeStruct(shape, bf16)...  2.23 us

profile of v5, /device:TPU:24, one launch (start us, length us, event | category | flops | bytes accessed | tf_op | source)
XLA Modules:
  0.0 45.4 jit_solution(15058317518050909393)
XLA Ops:
  0.6 42.5 %shard_map.84 = (bf16[128,8192]{1,0:T(8,128)(2,1)S(1)}, bf16[128,8192]{1,0:T(8,128)(2,1)S(1)}, bf16[128,1024]{1,0:T(8,128)(2,1)S(1)}, bf16[128,1024]{1,0:T(8,128)(2,1)S(1)}) custom-call(bf16[128,8192]{1,0:T(8,128)(2,1)} %q_hbm.1, bf16[128,1024]{1,0:T(8,128)(2,1)} %k_hbm.1, bf16[128,1024]{1,0:T(8,128)(2,1)} %v_hbm.1, bf16[128,8192]{1,0:T(8,128)(2,1)} %g_hbm.1, ...), custom_call_target="tpu_custom_call" | custom-call | tf_op jit(solution)/shard_map/pallas_call | solution.py:399
  43.1 2.2 %shard_map.85 = (bf16[128,8192]{1,0:T(8,128)(2,1)}, bf16[128,8192]{1,0:T(8,128)(2,1)}, bf16[128,1024]{1,0:T(8,128)(2,1)}, bf16[128,1024]{1,0:T(8,128)(2,1)}) custom-call(bf16[128,8192]{1,0:T(8,128)(2,1)S(1)} %get-tuple-element.8.refs_0_, bf16[128,8192]{1,0:T(8,128)(2,1)S(1)} %get-tuple-element.9.refs_1_, bf16[128,1024]{1,0:T(8,128)(2,1)S(1)} %get-tuple-element.10.refs_2_, ...), custom_call_target="tpu_custom_call" | custom-call | tf_op jit(solution)/shard_map/pallas_call | solution.py:420
